TPU v7x, 32 devices: a whole 2x2x4 slice. The times are simulated.
32 devices in a mesh: narrow: 4 (over z), wide: 8 (over y, x, core).
Axes of the slice: x: 2, y: 2, z: 4, core: 2. Of those that a mesh axis runs over, the one named last changes fastest.
Arguments:
- layer_in: bfloat16 [16384, 1024], P(('narrow', 'wide')), may hold values from -30 to 30
- first_values: bfloat16 [16384, 1024], P(('narrow', 'wide')), may hold values from -6 to 6
- out_grad: bfloat16 [16384, 1024], P(('narrow', 'wide')), may hold values from -6 to 6
- seq_group: int32 [32], P(('narrow', 'wide')), may hold values from 0 to 1
- short_split: int32 [32], P(('narrow', 'wide')), may hold values from 128 to 384
- attn_gain: bfloat16 [1024], P(('narrow', 'wide')), may hold values from 0.099609375 to 1.8984375
- mlp_gain: bfloat16 [1024], P(('narrow', 'wide')), may hold values from 0.099609375 to 1.8984375
- w_query: bfloat16 [1024, 1024], P(('narrow', 'wide')), may hold values from -0.1875 to 0.1875
- w_key: bfloat16 [1024, 1024], P(('narrow', 'wide')), may hold values from -0.1875 to 0.1875
- w_value: bfloat16 [1024, 1024], P(('narrow', 'wide')), may hold values from -0.1875 to 0.1875
- w_out: bfloat16 [1024, 1024], P(None, ('narrow', 'wide')), may hold values from -2 to 2
- w_gate: bfloat16 [1024, 2816], P('wide', 'narrow'), may hold values from -0.1875 to 0.1875
- w_up: bfloat16 [1024, 2816], P('wide', 'narrow'), may hold values from -0.1875 to 0.1875
- w_down: bfloat16 [2816, 1024], P('narrow', 'wide'), may hold values from -0.109375 to 0.109375
Outputs:
- layer_out: bfloat16 [16384, 1024], P(('narrow', 'wide'))
- in_grad: float32 [16384, 1024], P(('narrow', 'wide'))
- first_values_grad: float32 [16384, 1024], P(('narrow', 'wide'))
- attn_gain_grad: float32 [1024], P(('narrow', 'wide'))
- mlp_gain_grad: float32 [1024], P(('narrow', 'wide'))
- w_query_grad: float32 [1024, 1024], P(('narrow', 'wide'))
- w_key_grad: float32 [1024, 1024], P(('narrow', 'wide'))
- w_value_grad: float32 [1024, 1024], P(('narrow', 'wide'))
- w_out_grad: float32 [1024, 1024], P(None, ('narrow', 'wide'))
- w_gate_grad: float32 [1024, 2816], P('wide', 'narrow')
- w_up_grad: float32 [1024, 2816], P('wide', 'narrow')
- w_down_grad: float32 [2816, 1024], P('narrow', 'wide')
Inputs may be any that keep to these rules, and one draw needn't show every extreme that they name: `short_split`: used only in slots whose seq_group is 1.
All inputs are finite; a program needn't handle non-finite values.
Results may differ from a plain program's by a relative error of at most 0.014.
Values may be sent and summed in bfloat16 or wider, within the bound.
No kernel may reach another device: no remote copies, remote signals or barrier semaphores. Data moves between devices by JAX's collectives and lax.ppermute only.
A program may use at most 192 MiB of HBM per device.

v0:
```python
import math
import jax
import jax.numpy as jnp
from jax import lax
from jax.sharding import PartitionSpec as P

HEAD_DIM = 64
epsilon = 1e-06


def rms_scale(values):
    return lax.rsqrt(jnp.mean(values * values, axis=-1, keepdims=True) + epsilon)


def angles(positions, head_dim):
    half_dim = head_dim // 2
    frequency = jnp.exp(
        jnp.arange(half_dim, dtype=jnp.float32) * (-2.0 * math.log(10000.0) / head_dim)
    )
    turned = positions[:, None] * frequency[None, :]
    return (jnp.cos(turned)[:, None, :], jnp.sin(turned)[:, None, :])


def rotate(values, cos_table, sin_table):
    half_dim = values.shape[-1] // 2
    first_half = values[..., :half_dim]
    second_half = values[..., half_dim:]
    return jnp.concatenate(
        [
            first_half * cos_table - second_half * sin_table,
            second_half * cos_table + first_half * sin_table,
        ],
        axis=-1,
    )


def rotate_back(grads, cos_table, sin_table):
    half_dim = grads.shape[-1] // 2
    first_half = grads[..., :half_dim]
    second_half = grads[..., half_dim:]
    return jnp.concatenate(
        [
            first_half * cos_table + second_half * sin_table,
            second_half * cos_table - first_half * sin_table,
        ],
        axis=-1,
    )


def product(left, right):
    return jnp.dot(left, right, preferred_element_type=jnp.float32)


def norm_back(values, scale, gain_float, grad_normed):
    scaled = grad_normed * gain_float
    gain_grad = jnp.sum(grad_normed * values * scale, axis=0)
    grad_values = scale * scaled - values * (scale * scale * scale) * jnp.mean(
        scaled * values, axis=-1, keepdims=True
    )
    return (grad_values, gain_grad)


def silu_back(gate_proj, up_proj, grad_active):
    sigmoid_gate = jax.nn.sigmoid(gate_proj)
    grad_gate = (
        grad_active * up_proj * sigmoid_gate * (1.0 + gate_proj * (1.0 - sigmoid_gate))
    ).astype(jnp.bfloat16)
    grad_up = (grad_active * gate_proj * sigmoid_gate).astype(jnp.bfloat16)
    return (grad_gate, grad_up)


def on_device(
    layer_in,
    first_values,
    out_grad,
    seq_group,
    short_split,
    attn_gain,
    mlp_gain,
    w_query,
    w_key,
    w_value,
    w_out,
    w_gate,
    w_up,
    w_down,
):
    row_count, model_width = layer_in.shape
    head_dim = HEAD_DIM
    head_count = model_width // head_dim
    gain_attn, gain_mlp, full_query, full_key, full_value, full_out = (
        lax.all_gather(attn_gain, ("narrow", "wide"), axis=0, tiled=True),
        lax.all_gather(mlp_gain, ("narrow", "wide"), axis=0, tiled=True),
        lax.all_gather(w_query, ("narrow", "wide"), axis=0, tiled=True),
        lax.all_gather(w_key, ("narrow", "wide"), axis=0, tiled=True),
        lax.all_gather(w_value, ("narrow", "wide"), axis=0, tiled=True),
        lax.all_gather(w_out, ("narrow", "wide"), axis=1, tiled=True),
    )
    gate_cols, up_cols, down_rows = (
        lax.all_gather(w_gate, "wide", axis=0, tiled=True),
        lax.all_gather(w_up, "wide", axis=0, tiled=True),
        lax.all_gather(w_down, "wide", axis=1, tiled=True),
    )
    gain_attn = gain_attn.astype(jnp.float32)
    gain_mlp = gain_mlp.astype(jnp.float32)
    split_row = jnp.where(seq_group[0] == 0, row_count, short_split[0])
    row_index = jnp.arange(row_count, dtype=jnp.int32)
    second = row_index >= split_row
    positions = jnp.where(second, row_index - split_row, row_index).astype(jnp.float32)
    cos_table, sin_table = angles(positions, head_dim)
    input_rows = layer_in.astype(jnp.float32)
    scale_one = rms_scale(input_rows)
    normed = (input_rows * scale_one * gain_attn).astype(jnp.bfloat16)
    queries = rotate(
        product(normed, full_query).reshape(row_count, head_count, head_dim), cos_table, sin_table
    ).astype(jnp.bfloat16)
    key_rows = rotate(
        product(normed, full_key).reshape(row_count, head_count, head_dim), cos_table, sin_table
    ).astype(jnp.bfloat16)
    value_rows = (
        0.5 * product(normed, full_value) + 0.5 * first_values.astype(jnp.float32)
    ).astype(jnp.bfloat16)
    value_rows = value_rows.reshape(row_count, head_count, head_dim)
    block_rows = min(512, row_count)
    score_scale = head_dim ** (-0.5)

    def scores_for(row_block):
        query_start = row_block * block_rows
        key_end = query_start + block_rows
        raw_scores = (
            jnp.einsum("qhd,khd->hqk", queries, key_rows, preferred_element_type=jnp.float32)
            * score_scale
        )
        allowed = (second[query_start:key_end, None] == second[None, :key_end]) & (
            row_index[query_start:key_end, None] >= row_index[None, :key_end]
        )
        return jnp.where(allowed[None], raw_scores, -1e30)

    row_block = 0
    key_end = (row_block + 1) * block_rows
    scores = scores_for(row_block)
    row_max = jnp.max(scores, axis=-1, keepdims=True)
    exponent = jnp.exp(scores - row_max)
    row_sum = jnp.sum(exponent, axis=-1, keepdims=True)
    weights = (exponent / row_sum).astype(jnp.bfloat16)
    attended_parts = jnp.einsum(
        "hqk,khd->qhd", weights, value_rows, preferred_element_type=jnp.float32
    )
    log_sums = [row_max + jnp.log(row_sum)]
    attended = attended_parts.reshape(row_count, model_width).astype(jnp.bfloat16)
    hidden_in = input_rows + product(attended, full_out)
    scale_two = rms_scale(hidden_in)
    normed_two = (hidden_in * scale_two * gain_mlp).astype(jnp.bfloat16)
    gathered_rows = lax.all_gather(normed_two, "narrow", axis=0, tiled=True)
    gate_proj = product(gathered_rows, gate_cols)
    up_proj = product(gathered_rows, up_cols)
    active = (jax.nn.silu(gate_proj) * up_proj).astype(jnp.bfloat16)
    branch_out = lax.psum_scatter(
        product(active, down_rows).astype(jnp.bfloat16), "narrow", scatter_dimension=0, tiled=True
    ).astype(jnp.float32)
    grad_rows = lax.all_gather(out_grad, "narrow", axis=0, tiled=True)
    grad_active = product(grad_rows, down_rows.T)
    grad_down_w = product(active.T, grad_rows)
    grad_gate, grad_up = silu_back(gate_proj, up_proj, grad_active)
    grad_gate_w = product(gathered_rows.T, grad_gate)
    grad_up_w = product(gathered_rows.T, grad_up)
    grad_normed_two = lax.psum_scatter(
        product(grad_gate, gate_cols.T) + product(grad_up, up_cols.T),
        "narrow",
        scatter_dimension=0,
        tiled=True,
    )
    layer_out = (hidden_in + branch_out).astype(jnp.bfloat16)
    gate_grad, up_grad, down_grad = (
        lax.psum_scatter(
            grad_gate_w.astype(jnp.bfloat16), "wide", scatter_dimension=0, tiled=True
        ).astype(jnp.float32),
        lax.psum_scatter(
            grad_up_w.astype(jnp.bfloat16), "wide", scatter_dimension=0, tiled=True
        ).astype(jnp.float32),
        lax.psum_scatter(
            grad_down_w.astype(jnp.bfloat16), "wide", scatter_dimension=1, tiled=True
        ).astype(jnp.float32),
    )
    grad_norm_two, mlp_gain_part = norm_back(hidden_in, scale_two, gain_mlp, grad_normed_two)
    grad_hidden = out_grad.astype(jnp.float32) + grad_norm_two
    grad_branch = grad_hidden.astype(jnp.bfloat16)
    grad_out_w = product(attended.T, grad_branch)
    grad_attended = (
        product(grad_branch, full_out.T)
        .astype(jnp.bfloat16)
        .reshape(row_count, head_count, head_dim)
    )
    grad_keys = jnp.zeros((row_count, head_count, head_dim), jnp.float32)
    grad_values = jnp.zeros((row_count, head_count, head_dim), jnp.float32)
    row_block = 0
    query_start = row_block * block_rows
    key_end = query_start + block_rows
    scores = scores_for(row_block)
    probability = jnp.exp(scores - log_sums[row_block])
    grad_probs = jnp.einsum(
        "qhd,khd->hqk", grad_attended, value_rows, preferred_element_type=jnp.float32
    )
    delta_sum = jnp.sum(grad_probs * probability, axis=-1, keepdims=True)
    grad_scores = (score_scale * probability * (grad_probs - delta_sum)).astype(jnp.bfloat16)
    query_grad_parts = jnp.einsum(
        "hqk,khd->qhd", grad_scores, key_rows, preferred_element_type=jnp.float32
    )
    grad_keys = grad_keys.at[:key_end].add(
        jnp.einsum("hqk,qhd->khd", grad_scores, queries, preferred_element_type=jnp.float32)
    )
    grad_values = grad_values.at[:key_end].add(
        jnp.einsum(
            "hqk,qhd->khd",
            probability.astype(jnp.bfloat16),
            grad_attended,
            preferred_element_type=jnp.float32,
        )
    )
    grad_query_proj = (
        rotate_back(query_grad_parts, cos_table, sin_table)
        .reshape(row_count, model_width)
        .astype(jnp.bfloat16)
    )
    grad_key_proj = (
        rotate_back(grad_keys, cos_table, sin_table)
        .reshape(row_count, model_width)
        .astype(jnp.bfloat16)
    )
    values_grad = 0.5 * grad_values.reshape(row_count, model_width)
    grad_value_proj = values_grad.astype(jnp.bfloat16)
    grad_query_w = product(normed.T, grad_query_proj)
    grad_key_w = product(normed.T, grad_key_proj)
    grad_value_w = product(normed.T, grad_value_proj)
    grad_normed = (
        product(grad_query_proj, full_query.T)
        + product(grad_key_proj, full_key.T)
        + product(grad_value_proj, full_value.T)
    )
    grad_norm_one, attn_gain_part = norm_back(input_rows, scale_one, gain_attn, grad_normed)
    in_grad = grad_hidden + grad_norm_one
    attn_gain_grad, mlp_gain_grad, query_grad, key_grad, value_grad, out_proj_grad = (
        lax.psum_scatter(attn_gain_part, ("narrow", "wide"), scatter_dimension=0, tiled=True),
        lax.psum_scatter(mlp_gain_part, ("narrow", "wide"), scatter_dimension=0, tiled=True),
        lax.psum_scatter(grad_query_w, ("narrow", "wide"), scatter_dimension=0, tiled=True),
        lax.psum_scatter(grad_key_w, ("narrow", "wide"), scatter_dimension=0, tiled=True),
        lax.psum_scatter(grad_value_w, ("narrow", "wide"), scatter_dimension=0, tiled=True),
        lax.psum_scatter(grad_out_w, ("narrow", "wide"), scatter_dimension=1, tiled=True),
    )
    return (
        layer_out,
        in_grad,
        values_grad,
        attn_gain_grad,
        mlp_gain_grad,
        query_grad,
        key_grad,
        value_grad,
        out_proj_grad,
        gate_grad,
        up_grad,
        down_grad,
    )


def solution(mesh):
    placed = (
        P(("narrow", "wide"), None),
        P(("narrow", "wide"), None),
        P(("narrow", "wide"), None),
        P(("narrow", "wide")),
        P(("narrow", "wide")),
        P(("narrow", "wide")),
        P(("narrow", "wide")),
        P(("narrow", "wide"), None),
        P(("narrow", "wide"), None),
        P(("narrow", "wide"), None),
        P(None, ("narrow", "wide")),
        P("wide", "narrow"),
        P("wide", "narrow"),
        P("narrow", "wide"),
    )
    return jax.shard_map(
        on_device,
        mesh=mesh,
        in_specs=placed,
        out_specs=(
            P(("narrow", "wide"), None),
            P(("narrow", "wide"), None),
            P(("narrow", "wide"), None),
            P(("narrow", "wide")),
            P(("narrow", "wide")),
            P(("narrow", "wide"), None),
            P(("narrow", "wide"), None),
            P(("narrow", "wide"), None),
            P(None, ("narrow", "wide")),
            P("wide", "narrow"),
            P("wide", "narrow"),
            P("narrow", "wide"),
        ),
        check_vma=False,
    )
```

profile of v0, /device:TPU:0, one launch (start us, length us, event | category | flops | bytes accessed | tf_op | source)
XLA Modules:
  0.0 1429.1 jit_solution(4299515157416208333)
XLA Ops:
  15.2 42.0 %all-reduce.5 = (bf16[1024]{0:T(1024)(128)(2,1)S(1)}, bf16[1024]{0:T(1024)(128)(2,1)S(1)}) all-reduce(bf16[1024]{0:T(1024)(128)(2,1)S(1)} %dynamic-update-slice.4, bf16[1024]{0:T(1024)(128)(2,1)S(1)} %dynamic-update-slice.5), channel_id=1, replica_groups=mesh['narrow'=4,'wide'=8] {'narrow','wide'}, use_global_device_ids=true, to_apply=%add | all-reduce | flops 2048 | bytes 8192
  58.3 11.8 all-gather.10.cloned.1.call-done
  74.2 54.0 %all-gather.12.cloned.1.call-done = bf16[1024,1024]{1,0:T(8,128)(2,1)} async-done(((bf16[32,1024]{1,0:T(8,128)(2,1)}), bf16[1024,1024]{1,0:T(8,128)(2,1)}) %all-gather.12.cloned.1.call-update) | async-done | bytes 2097168 | tf_op jit(solution)/shard_map/all_gather | solution.py:94
  132.5 53.8 %all-gather.14.cloned.1.call-done = bf16[1024,1024]{1,0:T(8,128)(2,1)} async-done(((bf16[32,1024]{1,0:T(8,128)(2,1)}), bf16[1024,1024]{1,0:T(8,128)(2,1)}) %all-gather.14.cloned.1.call-update) | async-done | bytes 2097168 | tf_op jit(solution)/shard_map/all_gather | solution.py:95
  205.9 8.7 fusion.18
  214.6 29.7 %all-gather.16.cloned.1.call-done = bf16[1024,1024]{0,1:T(8,128)(2,1)} async-done(((bf16[1024,32]{0,1:T(8,128)(2,1)}), bf16[1024,1024]{0,1:T(8,128)(2,1)}) %all-gather.16.cloned.1.call-update) | async-done | bytes 2097168 | tf_op jit(solution)/shard_map/all_gather | solution.py:97
  251.3 18.9 %all-gather.22.cloned.1.call-done = bf16[1024,704]{0,1:T(8,128)(2,1)} async-done(((bf16[128,704]{0,1:T(8,128)(2,1)}), bf16[1024,704]{0,1:T(8,128)(2,1)}) %all-gather.22.cloned.1.call-update) | async-done | bytes 1441808 | tf_op jit(solution)/shard_map/all_gather | solution.py:101
  270.2 82.8 %all-gather.18.cloned.1.call-done = bf16[2048,1024]{1,0:T(8,128)(2,1)} async-done(((bf16[512,1024]{1,0:T(8,128)(2,1)}), bf16[2048,1024]{1,0:T(8,128)(2,1)}) %all-gather.18.cloned.1.call-update) | async-done | bytes 4194320 | tf_op jit(solution)/shard_map/all_gather | solution.py:154
  361.3 17.4 %all-gather.20.cloned.1.call-done = bf16[1024,704]{0,1:T(8,128)(2,1)} async-done(((bf16[128,704]{0,1:T(8,128)(2,1)}), bf16[1024,704]{0,1:T(8,128)(2,1)}) %all-gather.20.cloned.1.call-update) | async-done | bytes 1441808 | tf_op jit(solution)/shard_map/all_gather | solution.py:100
  378.7 8.3 fusion.40
  387.0 18.9 %all-gather.24.cloned.1.call-done = bf16[704,1024]{1,0:T(8,128)(2,1)} async-done(((bf16[704,128]{1,0:T(8,128)(2,1)}), bf16[704,1024]{1,0:T(8,128)(2,1)}) %all-gather.24.cloned.1.call-update) | async-done | bytes 1441808 | tf_op jit(solution)/shard_map/all_gather | solution.py:102
  405.9 82.4 %all-gather.26.cloned.1.call-done = bf16[2048,1024]{1,0:T(8,128)(2,1)} async-done(((bf16[512,1024]{1,0:T(8,128)(2,1)}), bf16[2048,1024]{1,0:T(8,128)(2,1)}) %all-gather.26.cloned.1.call-update) | async-done | bytes 4194320 | tf_op jit(solution)/shard_map/all_gather | solution.py:161
  488.3 12.1 multiply_convert_fusion.1
  547.7 105.2 %reduce-scatter.18.cloned.1.call-done = f32[512,1024]{1,0:T(8,128)} async-done(((f32[2048,1024]{1,0:T(8,128)}), f32[512,1024]{1,0:T(8,128)}) %reduce-scatter.18.cloned.1.call-update) | async-done | bytes 2097168 | tf_op jit(solution)/shard_map/reduce_scatter | solution.py:167
  655.1 77.7 %reduce-scatter.16.cloned.1.call-done = bf16[512,1024]{1,0:T(8,128)(2,1)} async-done(((bf16[2048,1024]{1,0:T(8,128)(2,1)}), bf16[512,1024]{1,0:T(8,128)(2,1)}) %reduce-scatter.16.cloned.1.call-update) | async-done | bytes 1048592 | tf_op jit(solution)/shard_map/reduce_scatter | solution.py:158
  759.1 8.5 multiply_reduce_fusion
  767.6 8.4 multiply_convert_fusion
  793.0 24.4 %reduce-scatter.30.cloned.1.call-done = bf16[128,704]{1,0:T(8,128)(2,1)} async-done(((bf16[1024,704]{1,0:T(8,128)(2,1)}), bf16[128,704]{1,0:T(8,128)(2,1)}) %reduce-scatter.30.cloned.1.call-update) | async-done | bytes 180240
  819.3 40.1 %reduce-scatter.28.cloned.1.call-done = bf16[128,704]{1,0:T(8,128)(2,1)} async-done(((bf16[1024,704]{1,0:T(8,128)(2,1)}), bf16[128,704]{1,0:T(8,128)(2,1)}) %reduce-scatter.28.cloned.1.call-update) | async-done | bytes 180240
  871.2 39.8 %all-reduce.4 = (f32[1024]{0:T(1024)S(1)}, f32[1024]{0:T(1024)S(1)}) all-reduce(f32[1024]{0:T(1024)S(1)} %get-tuple-element.90, f32[1024]{0:T(1024)S(1)} %get-tuple-element.88), channel_id=4, replica_groups=mesh['narrow'=4,'wide'=8] {'narrow','wide'}, use_global_device_ids=true, to_apply=%region_10.11.clone | all-reduce | flops 2048 | bytes 16384
  916.3 86.8 %reduce-scatter.26.cloned.1.call-done = f32[1024,32]{0,1:T(8,128)} async-done(((f32[1024,1024]{0,1:T(8,128)}), f32[1024,32]{0,1:T(8,128)}) %reduce-scatter.26.cloned.1.call-update) | async-done | bytes 131088 | tf_op jit(solution)/shard_map/reduce_scatter | solution.py:248
  1003.1 139.6 %reduce-scatter.24.cloned.1.call-done = f32[32,1024]{1,0:T(8,128)} async-done(((f32[1024,1024]{1,0:T(8,128)}), f32[32,1024]{1,0:T(8,128)}) %reduce-scatter.24.cloned.1.call-update) | async-done | bytes 131088 | tf_op jit(solution)/shard_map/reduce_scatter | solution.py:247
  1142.7 139.6 %reduce-scatter.20.cloned.1.call-done = f32[32,1024]{1,0:T(8,128)} async-done(((f32[1024,1024]{1,0:T(8,128)}), f32[32,1024]{1,0:T(8,128)}) %reduce-scatter.20.cloned.1.call-update) | async-done | bytes 131088 | tf_op jit(solution)/shard_map/reduce_scatter | solution.py:245
  1282.3 139.5 %reduce-scatter.22.cloned.1.call-done = f32[32,1024]{1,0:T(8,128)} async-done(((f32[1024,1024]{1,0:T(8,128)}), f32[32,1024]{1,0:T(8,128)}) %reduce-scatter.22.cloned.1.call-update) | async-done | bytes 131088 | tf_op jit(solution)/shard_map/reduce_scatter | solution.py:246
  (161 shorter events, 162.2 us)
Async XLA Ops:
  7.2 62.9 %all-gather.10.cloned.1.call-start = ((), (), s32[]{:S(2)}) async-start(), calls=%async_computation.9 | async-start | bytes 2162688 | tf_op jit(solution)/shard_map/all_gather | solution.py:96
  7.9 120.3 %all-gather.12.cloned.1.call-start = ((), (), s32[]{:S(2)}) async-start(), calls=%async_computation.10 | async-start | bytes 2162688 | tf_op jit(solution)/shard_map/all_gather | solution.py:94
  8.7 177.6 %all-gather.14.cloned.1.call-start = ((), (), s32[]{:S(2)}) async-start(), calls=%async_computation.11 | async-start | bytes 2162688 | tf_op jit(solution)/shard_map/all_gather | solution.py:95
  9.4 234.9 %all-gather.16.cloned.1.call-start = ((), (), s32[]{:S(2)}) async-start(), calls=%async_computation.12 | async-start | bytes 2162688 | tf_op jit(solution)/shard_map/all_gather | solution.py:97
  10.0 260.2 %all-gather.22.cloned.1.call-start = ((), (), s32[]{:S(2)}) async-start(), calls=%async_computation.15 | async-start | bytes 1622016 | tf_op jit(solution)/shard_map/all_gather | solution.py:101
  10.6 342.4 %all-gather.18.cloned.1.call-start = ((), (), s32[]{:S(2)}) async-start(), calls=%async_computation.13 | async-start | bytes 5242880 | tf_op jit(solution)/shard_map/all_gather | solution.py:154
  58.3 131.2 %copy-start.21 = (f32[512,32]{0,1:T(8,128)}, f32[512,32]{0,1:T(8,128)S(1)}, u32[]{:S(2)}) copy-start(f32[512,32]{0,1:T(8,128)S(1)} %get-tuple-element.113) | copy-start | bytes 196612
  58.3 131.2 %copy-start.23 = (f32[512,32]{0,1:T(8,128)}, f32[512,32]{0,1:T(8,128)S(1)}, u32[]{:S(2)}) copy-start(f32[512,32]{0,1:T(8,128)S(1)} %get-tuple-element.114) | copy-start | bytes 196612
  70.1 58.1 %copy-start.2 = (bf16[512,1024]{1,0:T(8,128)(2,1)S(1)}, bf16[512,1024]{1,0:T(8,128)(2,1)}, u32[]{:S(2)}) copy-start(bf16[512,1024]{1,0:T(8,128)(2,1)} %param.22) | copy-start | bytes 3145732
  74.2 131.8 %copy-start.7 = (bf16[512,1024]{0,1:T(8,128)(2,1)}, bf16[512,1024]{0,1:T(8,128)(2,1)S(1)}, u32[]{:S(2)}) copy-start(bf16[512,1024]{0,1:T(8,128)(2,1)S(1)} %copy.48) | copy-start | bytes 3145732
  247.6 405.4 %copy-start.5 = (f32[512,1024]{1,0:T(8,128)}, f32[512,1024]{1,0:T(8,128)S(1)}, u32[]{:S(2)}) copy-start(f32[512,1024]{1,0:T(8,128)S(1)} %get-tuple-element.122) | copy-start | bytes 6291460
  249.0 129.7 %all-gather.20.cloned.1.call-start = ((), (), s32[]{:S(2)}) async-start(), calls=%async_computation.14 | async-start | bytes 1622016 | tf_op jit(solution)/shard_map/all_gather | solution.py:100
  249.8 156.1 %all-gather.24.cloned.1.call-start = ((), (), s32[]{:S(2)}) async-start(), calls=%async_computation.16 | async-start | bytes 1622016 | tf_op jit(solution)/shard_map/all_gather | solution.py:102
  250.5 237.8 %all-gather.26.cloned.1.call-start = ((), (), s32[]{:S(2)}) async-start(), calls=%async_computation.18 | async-start | bytes 5242880 | tf_op jit(solution)/shard_map/all_gather | solution.py:161
  251.3 401.7 %reduce-scatter.18.cloned.1.call-start = ((), (), s32[]{:S(2)}) async-start(), calls=%async_computation.19 | async-start | bytes 10485760 | tf_op jit(solution)/shard_map/reduce_scatter | solution.py:167
  509.8 223.0 %reduce-scatter.16.cloned.1.call-start = ((), (), s32[]{:S(2)}) async-start(), calls=%async_computation.17 | async-start | bytes 5242880 | tf_op jit(solution)/shard_map/reduce_scatter | solution.py:158
  517.5 273.5 %reduce-scatter.32.cloned.1.call-start = ((), (), s32[]{:S(2)}) async-start(), calls=%async_computation.26 | async-start | bytes 1769472
  527.7 289.8 %reduce-scatter.30.cloned.1.call-start = ((), (), s32[]{:S(2)}) async-start(), calls=%async_computation.25 | async-start | bytes 1769472
  537.7 321.7 %reduce-scatter.28.cloned.1.call-start = ((), (), s32[]{:S(2)}) async-start(), calls=%async_computation.24 | async-start | bytes 1769472
  547.7 455.4 %reduce-scatter.26.cloned.1.call-start = ((), (), s32[]{:S(2)}) async-start(), calls=%async_computation.23 | async-start | bytes 4325376 | tf_op jit(solution)/shard_map/reduce_scatter | solution.py:248
  740.6 402.0 %reduce-scatter.24.cloned.1.call-start = ((), (), s32[]{:S(2)}) async-start(), calls=%async_computation.22 | async-start | bytes 4325376 | tf_op jit(solution)/shard_map/reduce_scatter | solution.py:247
  759.1 523.3 %reduce-scatter.20.cloned.1.call-start = ((), (), s32[]{:S(2)}) async-start(), calls=%async_computation.20 | async-start | bytes 4325376 | tf_op jit(solution)/shard_map/reduce_scatter | solution.py:245
  787.1 634.7 %reduce-scatter.22.cloned.1.call-start = ((), (), s32[]{:S(2)}) async-start(), calls=%async_computation.21 | async-start | bytes 4325376 | tf_op jit(solution)/shard_map/reduce_scatter | solution.py:246
  791.0 70.3 %copy-start.1 = (f32[16,64,512]{2,1,0:T(8,128)S(1)}, f32[16,64,512]{2,1,0:T(8,128)}, u32[]{:S(2)}) copy-start(f32[16,64,512]{2,1,0:T(8,128)} %copy-done) | copy-start | bytes 6291460
  (25 other events, 152.3 us)
Sparse Core Ops, SparseCore 0:
  10.9 59.1 all-gather.9
  72.9 55.2 all-gather.11
  131.0 55.2 all-gather.13
  189.0 55.2 all-gather.15
  246.0 24.1 all-gather.21
  272.2 80.7 all-gather.17
  354.9 23.8 all-gather.19
  380.6 25.2 all-gather.23
  407.5 80.7 all-gather.25
  509.9 142.9 reduce-scatter.17
  655.3 77.4 reduce-scatter.15
  736.3 38.9 reduce-scatter.31
  778.9 38.4 reduce-scatter.29
  820.9 38.4 reduce-scatter.27
  862.2 140.8 reduce-scatter.25
  1005.9 136.7 reduce-scatter.23
  1145.5 136.8 reduce-scatter.19
  1285.1 136.6 reduce-scatter.21
where the time goes:
time: 1440 us; the launch traced here: 1430 us
  waiting for transfers between devices  1130 us (78%)
  matrix products  145 us (10%)
  blocking collectives  81.8 us (6%)
  other arithmetic  35.4 us (2%)
  local copies, waits for them, and re-layouts  21 us (1%)
  between operations  16.6 us (1%)
    reduce_scatter x1, waiting for transfers between devices, on_device(): lax.psum_scatter(grad_query_w, ('narrow', 'wide'), scatter_dimension=0, t...  140 us
    reduce_scatter x1, waiting for transfers between devices, on_device(): lax.psum_scatter(grad_value_w, ('narrow', 'wide'), scatter_dimension=0, t...  140 us
    reduce_scatter x1, waiting for transfers between devices, on_device(): lax.psum_scatter(grad_key_w, ('narrow', 'wide'), scatter_dimension=0, til...  139 us
    dot_general x21, matrix products, product(): return jnp.dot(left, right, preferred_element_type=jnp.float32)  107 us
    reduce_scatter x1, waiting for transfers between devices, on_device(): lax.psum_scatter(product(grad_gate, gate_cols.T) + product(grad_up, up_co...  105 us
    reduce_scatter x1, waiting for transfers between devices, on_device(): lax.psum_scatter(grad_out_w, ('narrow', 'wide'), scatter_dimension=1, til...  86.8 us
    all_gather x1, waiting for transfers between devices, on_device(): gathered_rows = lax.all_gather(normed_two, 'narrow', axis=0, tiled=True)  82.8 us
    all_gather x1, waiting for transfers between devices, on_device(): grad_rows = lax.all_gather(out_grad, 'narrow', axis=0, tiled=True)  82.4 us
  transfers between devices with their start and end apart: 18, of which 17 were waited for; matrix products, arithmetic and copies ran while one was open for 12% of the time, Pallas kernels for 0%

commit v1 on v0

--- a/solution.py
+++ b/solution.py
@@ -6,6 +6,12 @@
 
 HEAD_DIM = 64
 epsilon = 1e-06
+
+
+def joined_along(blocks, dim):
+    blocks = jnp.moveaxis(blocks, 0, dim)
+    shape = blocks.shape
+    return blocks.reshape(*shape[:dim], shape[dim] * shape[dim + 1], *shape[dim + 2 :])
 
 
 def rms_scale(values):
@@ -158,7 +164,19 @@
     branch_out = lax.psum_scatter(
         product(active, down_rows).astype(jnp.bfloat16), "narrow", scatter_dimension=0, tiled=True
     ).astype(jnp.float32)
-    grad_rows = lax.all_gather(out_grad, "narrow", axis=0, tiled=True)
+    count = lax.axis_size("narrow")
+    pairs = [(i, (i + 1) % count) for i in range(count)]
+    back = [(b, a) for a, b in pairs]
+    lower, upper = ([], [])
+    for step in range(count - 1):
+        if step % 2 == 0:
+            lower.append(lax.ppermute(lower[-1] if lower else out_grad, "narrow", pairs))
+        else:
+            upper.append(lax.ppermute(upper[-1] if upper else out_grad, "narrow", back))
+    pieces = jnp.stack([*lower[::-1], out_grad, *upper])
+    shift = lax.axis_index("narrow") - len(lower)
+    pieces = pieces[(jnp.arange(count) - shift) % count]
+    grad_rows = joined_along(pieces, 0)
     grad_active = product(grad_rows, down_rows.T)
     grad_down_w = product(active.T, grad_rows)
     grad_gate, grad_up = silu_back(gate_proj, up_proj, grad_active)

time: 1440 us -> 1390 us (0.965)
  waiting for transfers between devices: 1130 us -> 1070 us
    ppermute x0 -> x3, waiting for transfers between devices: none -> 106 us  [the longest x1 65.8 us: on_device(): upper.append(lax.ppermute(upper[-1] if upper else out_grad, 'narrow', back))]
    all_gather x1 -> x0, waiting for transfers between devices: 82.4 us -> none  [on_device(): grad_rows = lax.all_gather(out_grad, 'narrow', axis=0, tiled=True)]
    all_gather x1, waiting for transfers between devices: 82.8 us -> 20.4 us  [on_device(): gathered_rows = lax.all_gather(normed_two, 'narrow', axis=0, tiled=True)]
    all_gather x1, waiting for transfers between devices: 18.9 us -> 0.01 us  [on_device(): lax.all_gather(w_up, 'wide', axis=0, tiled=True)]
    unnamed x21 -> x20, waiting for transfers between devices: 69.9 us -> 68.3 us
  transfers between devices with their start and end apart: 18 -> 20, of which waited for: 17 -> 18; matrix products, arithmetic and copies ran while one was open for 12% -> 13% of each run, Pallas kernels for 0% -> 0%
where the time goes in v1:
time: 1390 us; the launch traced here: 1380 us
  waiting for transfers between devices  1070 us (77%)
  matrix products  146 us (11%)
  blocking collectives  81.7 us (6%)
  other arithmetic  39.1 us (3%)
  local copies, waits for them, and re-layouts  25 us (2%)
  between operations  16.3 us (1%)
    reduce_scatter x1, waiting for transfers between devices, on_device(): lax.psum_scatter(grad_query_w, ('narrow', 'wide'), scatter_dimension=0, t...  140 us
    reduce_scatter x1, waiting for transfers between devices, on_device(): lax.psum_scatter(grad_key_w, ('narrow', 'wide'), scatter_dimension=0, til...  140 us
    reduce_scatter x1, waiting for transfers between devices, on_device(): lax.psum_scatter(grad_value_w, ('narrow', 'wide'), scatter_dimension=0, t...  140 us
    dot_general x21, matrix products, product(): return jnp.dot(left, right, preferred_element_type=jnp.float32)  109 us
    reduce_scatter x1, waiting for transfers between devices, on_device(): lax.psum_scatter(product(grad_gate, gate_cols.T) + product(grad_up, up_co...  107 us
    reduce_scatter x1, waiting for transfers between devices, on_device(): lax.psum_scatter(grad_out_w, ('narrow', 'wide'), scatter_dimension=1, til...  87 us
    unnamed x2, blocking collectives  81.7 us
    reduce_scatter x1, waiting for transfers between devices, on_device(): lax.psum_scatter(product(active, down_rows).astype(jnp.bfloat16), 'narrow...  77.5 us
  transfers between devices with their start and end apart: 20, of which 18 were waited for; matrix products, arithmetic and copies ran while one was open for 13% of the time, Pallas kernels for 0%

profile of v1, /device:TPU:0, one launch (start us, length us, event | category | flops | bytes accessed | tf_op | source)
XLA Modules:
  0.0 1384.3 jit_solution(16154939046078821957)
XLA Ops:
  15.2 42.0 %all-reduce.5 = (bf16[1024]{0:T(1024)(128)(2,1)S(1)}, bf16[1024]{0:T(1024)(128)(2,1)S(1)}) all-reduce(bf16[1024]{0:T(1024)(128)(2,1)S(1)} %dynamic-update-slice.4, bf16[1024]{0:T(1024)(128)(2,1)S(1)} %dynamic-update-slice.5), channel_id=1, replica_groups=mesh['narrow'=4,'wide'=8] {'narrow','wide'}, use_global_device_ids=true, to_apply=%add | all-reduce | flops 2048 | bytes 8192
  58.3 11.8 all-gather.9.cloned.1.call-done
  74.2 54.0 %all-gather.11.cloned.1.call-done = bf16[1024,1024]{1,0:T(8,128)(2,1)} async-done(((bf16[32,1024]{1,0:T(8,128)(2,1)}), bf16[1024,1024]{1,0:T(8,128)(2,1)}) %all-gather.11.cloned.1.call-update) | async-done | bytes 2097168 | tf_op jit(solution)/shard_map/all_gather | solution.py:100
  132.5 53.8 %all-gather.13.cloned.1.call-done = bf16[1024,1024]{1,0:T(8,128)(2,1)} async-done(((bf16[32,1024]{1,0:T(8,128)(2,1)}), bf16[1024,1024]{1,0:T(8,128)(2,1)}) %all-gather.13.cloned.1.call-update) | async-done | bytes 2097168 | tf_op jit(solution)/shard_map/all_gather | solution.py:101
  205.9 8.8 fusion.18
  214.8 29.5 %all-gather.15.cloned.1.call-done = bf16[1024,1024]{0,1:T(8,128)(2,1)} async-done(((bf16[1024,32]{0,1:T(8,128)(2,1)}), bf16[1024,1024]{0,1:T(8,128)(2,1)}) %all-gather.15.cloned.1.call-update) | async-done | bytes 2097168 | tf_op jit(solution)/shard_map/all_gather | solution.py:103
  253.5 24.3 %collective-permute-done = bf16[512,1024]{1,0:T(8,128)(2,1)} collective-permute-done((bf16[512,1024]{1,0:T(8,128)(2,1)}, bf16[512,1024]{1,0:T(8,128)(2,1)}, u32[]{:S(2)}, u32[]{:S(2)}) %collective-permute-start) | collective-permute-done | bytes 1048608 | tf_op jit(solution)/shard_map/ppermute | solution.py:173
  278.0 65.8 %collective-permute-done.2 = bf16[512,1024]{1,0:T(8,128)(2,1)} collective-permute-done((bf16[512,1024]{1,0:T(8,128)(2,1)}, bf16[512,1024]{1,0:T(8,128)(2,1)}, u32[]{:S(2)}, u32[]{:S(2)}) %collective-permute-start.2) | collective-permute-done | bytes 1048608 | tf_op jit(solution)/shard_map/ppermute | solution.py:175
  343.8 15.9 %collective-permute-done.1 = bf16[512,1024]{1,0:T(8,128)(2,1)} collective-permute-done((bf16[512,1024]{1,0:T(8,128)(2,1)}, bf16[512,1024]{1,0:T(8,128)(2,1)}, u32[]{:S(2)}, u32[]{:S(2)}) %collective-permute-start.1) | collective-permute-done | bytes 1048608 | tf_op jit(solution)/shard_map/ppermute | solution.py:173
  368.5 20.4 %all-gather.17.cloned.1.call-done = bf16[2048,1024]{1,0:T(8,128)(2,1)} async-done(((bf16[512,1024]{1,0:T(8,128)(2,1)}), bf16[2048,1024]{1,0:T(8,128)(2,1)}) %all-gather.17.cloned.1.call-update) | async-done | bytes 4194320 | tf_op jit(solution)/shard_map/all_gather | solution.py:160
  397.2 17.4 %all-gather.19.cloned.1.call-done = bf16[1024,704]{0,1:T(8,128)(2,1)} async-done(((bf16[128,704]{0,1:T(8,128)(2,1)}), bf16[1024,704]{0,1:T(8,128)(2,1)}) %all-gather.19.cloned.1.call-update) | async-done | bytes 1441808 | tf_op jit(solution)/shard_map/all_gather | solution.py:106
  422.9 18.9 %all-gather.23.cloned.1.call-done = bf16[704,1024]{1,0:T(8,128)(2,1)} async-done(((bf16[704,128]{1,0:T(8,128)(2,1)}), bf16[704,1024]{1,0:T(8,128)(2,1)}) %all-gather.23.cloned.1.call-update) | async-done | bytes 1441808 | tf_op jit(solution)/shard_map/all_gather | solution.py:108
  441.8 11.8 multiply_convert_fusion.1
  501.0 106.8 %reduce-scatter.18.cloned.1.call-done = f32[512,1024]{1,0:T(8,128)} async-done(((f32[2048,1024]{1,0:T(8,128)}), f32[512,1024]{1,0:T(8,128)}) %reduce-scatter.18.cloned.1.call-update) | async-done | bytes 2097168 | tf_op jit(solution)/shard_map/reduce_scatter | solution.py:185
  609.9 77.5 %reduce-scatter.16.cloned.1.call-done = bf16[512,1024]{1,0:T(8,128)(2,1)} async-done(((bf16[2048,1024]{1,0:T(8,128)(2,1)}), bf16[512,1024]{1,0:T(8,128)(2,1)}) %reduce-scatter.16.cloned.1.call-update) | async-done | bytes 1048592 | tf_op jit(solution)/shard_map/reduce_scatter | solution.py:164
  714.2 8.5 multiply_reduce_fusion
  722.6 8.4 multiply_convert_fusion
  748.1 24.0 %reduce-scatter.30.cloned.1.call-done = bf16[128,704]{1,0:T(8,128)(2,1)} async-done(((bf16[1024,704]{1,0:T(8,128)(2,1)}), bf16[128,704]{1,0:T(8,128)(2,1)}) %reduce-scatter.30.cloned.1.call-update) | async-done | bytes 180240
  774.0 40.3 %reduce-scatter.28.cloned.1.call-done = bf16[128,704]{1,0:T(8,128)(2,1)} async-done(((bf16[1024,704]{1,0:T(8,128)(2,1)}), bf16[128,704]{1,0:T(8,128)(2,1)}) %reduce-scatter.28.cloned.1.call-update) | async-done | bytes 180240
  826.1 39.8 %all-reduce.4 = (f32[1024]{0:T(1024)S(1)}, f32[1024]{0:T(1024)S(1)}) all-reduce(f32[1024]{0:T(1024)S(1)} %get-tuple-element.90, f32[1024]{0:T(1024)S(1)} %get-tuple-element.88), channel_id=4, replica_groups=mesh['narrow'=4,'wide'=8] {'narrow','wide'}, use_global_device_ids=true, to_apply=%region_10.11.clone | all-reduce | flops 2048 | bytes 16384
  871.1 87.0 %reduce-scatter.26.cloned.1.call-done = f32[1024,32]{0,1:T(8,128)} async-done(((f32[1024,1024]{0,1:T(8,128)}), f32[1024,32]{0,1:T(8,128)}) %reduce-scatter.26.cloned.1.call-update) | async-done | bytes 131088 | tf_op jit(solution)/shard_map/reduce_scatter | solution.py:266
  958.2 139.5 %reduce-scatter.24.cloned.1.call-done = f32[32,1024]{1,0:T(8,128)} async-done(((f32[1024,1024]{1,0:T(8,128)}), f32[32,1024]{1,0:T(8,128)}) %reduce-scatter.24.cloned.1.call-update) | async-done | bytes 131088 | tf_op jit(solution)/shard_map/reduce_scatter | solution.py:265
  1097.7 139.8 %reduce-scatter.20.cloned.1.call-done = f32[32,1024]{1,0:T(8,128)} async-done(((f32[1024,1024]{1,0:T(8,128)}), f32[32,1024]{1,0:T(8,128)}) %reduce-scatter.20.cloned.1.call-update) | async-done | bytes 131088 | tf_op jit(solution)/shard_map/reduce_scatter | solution.py:263
  1237.6 139.7 %reduce-scatter.22.cloned.1.call-done = f32[32,1024]{1,0:T(8,128)} async-done(((f32[1024,1024]{1,0:T(8,128)}), f32[32,1024]{1,0:T(8,128)}) %reduce-scatter.22.cloned.1.call-update) | async-done | bytes 131088 | tf_op jit(solution)/shard_map/reduce_scatter | solution.py:264
  (164 shorter events, 182.2 us)
Async XLA Ops:
  7.2 62.9 %all-gather.9.cloned.1.call-start = ((), (), s32[]{:S(2)}) async-start(), calls=%async_computation.9 | async-start | bytes 2162688 | tf_op jit(solution)/shard_map/all_gather | solution.py:102
  7.9 120.3 %all-gather.11.cloned.1.call-start = ((), (), s32[]{:S(2)}) async-start(), calls=%async_computation.10 | async-start | bytes 2162688 | tf_op jit(solution)/shard_map/all_gather | solution.py:100
  8.7 177.7 %all-gather.13.cloned.1.call-start = ((), (), s32[]{:S(2)}) async-start(), calls=%async_computation.11 | async-start | bytes 2162688 | tf_op jit(solution)/shard_map/all_gather | solution.py:101
  9.4 234.9 %all-gather.15.cloned.1.call-start = ((), (), s32[]{:S(2)}) async-start(), calls=%async_computation.12 | async-start | bytes 2162688 | tf_op jit(solution)/shard_map/all_gather | solution.py:103
  10.0 358.6 %all-gather.21.cloned.1.call-start = ((), (), s32[]{:S(2)}) async-start(), calls=%async_computation.15 | async-start | bytes 1622016 | tf_op jit(solution)/shard_map/all_gather | solution.py:107
  10.6 378.4 %all-gather.17.cloned.1.call-start = ((), (), s32[]{:S(2)}) async-start(), calls=%async_computation.13 | async-start | bytes 5242880 | tf_op jit(solution)/shard_map/all_gather | solution.py:160
  58.3 131.2 %copy-start.19 = (f32[512,32]{0,1:T(8,128)}, f32[512,32]{0,1:T(8,128)S(1)}, u32[]{:S(2)}) copy-start(f32[512,32]{0,1:T(8,128)S(1)} %get-tuple-element.113) | copy-start | bytes 196612
  58.3 131.2 %copy-start.21 = (f32[512,32]{0,1:T(8,128)}, f32[512,32]{0,1:T(8,128)S(1)}, u32[]{:S(2)}) copy-start(f32[512,32]{0,1:T(8,128)S(1)} %get-tuple-element.114) | copy-start | bytes 196612
  74.2 131.8 %copy-start.5 = (bf16[512,1024]{0,1:T(8,128)(2,1)}, bf16[512,1024]{0,1:T(8,128)(2,1)S(1)}, u32[]{:S(2)}) copy-start(bf16[512,1024]{0,1:T(8,128)(2,1)S(1)} %copy.48) | copy-start | bytes 3145732
  248.9 165.7 %all-gather.19.cloned.1.call-start = ((), (), s32[]{:S(2)}) async-start(), calls=%async_computation.14 | async-start | bytes 1622016 | tf_op jit(solution)/shard_map/all_gather | solution.py:106
  249.6 192.2 %all-gather.23.cloned.1.call-start = ((), (), s32[]{:S(2)}) async-start(), calls=%async_computation.16 | async-start | bytes 1622016 | tf_op jit(solution)/shard_map/all_gather | solution.py:108
  249.7 28.2 %collective-permute-start = (bf16[512,1024]{1,0:T(8,128)(2,1)}, bf16[512,1024]{1,0:T(8,128)(2,1)}, u32[]{:S(2)}, u32[]{:S(2)}) collective-permute-start(bf16[512,1024]{1,0:T(8,128)(2,1)} %param.24), channel_id=1, source_target_pairs={{0,8},{8,16},{16,24},{24,0},{1,9},{9,17},{17,25},{25,1},{2,10},{10... | collective-permute-start | bytes 3145736 | tf_op jit(solution)/shard_map/ppermute | solution.py:173
  250.3 93.5 %collective-permute-start.2 = (bf16[512,1024]{1,0:T(8,128)(2,1)}, bf16[512,1024]{1,0:T(8,128)(2,1)}, u32[]{:S(2)}, u32[]{:S(2)}) collective-permute-start(bf16[512,1024]{1,0:T(8,128)(2,1)} %param.24), channel_id=1, source_target_pairs={{8,0},{16,8},{24,16},{0,24},{9,1},{17,9},{25,17},{1,25},{10,2},{18... | collective-permute-start | bytes 3145736 | tf_op jit(solution)/shard_map/ppermute | solution.py:175
  277.9 81.9 %collective-permute-start.1 = (bf16[512,1024]{1,0:T(8,128)(2,1)}, bf16[512,1024]{1,0:T(8,128)(2,1)}, u32[]{:S(2)}, u32[]{:S(2)}) collective-permute-start(bf16[512,1024]{1,0:T(8,128)(2,1)} %collective-permute-done), channel_id=1, source_target_pairs={{0,8},{8,16},{16,24},{24,0},{1,9},{9,17},{17,25},{25,1},{2,10},{10... | collective-permute-start | bytes 3145736 | tf_op jit(solution)/shard_map/ppermute | solution.py:173
  277.9 329.9 %reduce-scatter.18.cloned.1.call-start = ((), (), s32[]{:S(2)}) async-start(), calls=%async_computation.18 | async-start | bytes 10485760 | tf_op jit(solution)/shard_map/reduce_scatter | solution.py:185
  463.2 224.3 %reduce-scatter.16.cloned.1.call-start = ((), (), s32[]{:S(2)}) async-start(), calls=%async_computation.17 | async-start | bytes 5242880 | tf_op jit(solution)/shard_map/reduce_scatter | solution.py:164
  470.9 275.2 %reduce-scatter.32.cloned.1.call-start = ((), (), s32[]{:S(2)}) async-start(), calls=%async_computation.25 | async-start | bytes 1769472
  480.9 291.3 %reduce-scatter.30.cloned.1.call-start = ((), (), s32[]{:S(2)}) async-start(), calls=%async_computation.24 | async-start | bytes 1769472
  490.8 323.4 %reduce-scatter.28.cloned.1.call-start = ((), (), s32[]{:S(2)}) async-start(), calls=%async_computation.23 | async-start | bytes 1769472
  501.0 457.2 %reduce-scatter.26.cloned.1.call-start = ((), (), s32[]{:S(2)}) async-start(), calls=%async_computation.22 | async-start | bytes 4325376 | tf_op jit(solution)/shard_map/reduce_scatter | solution.py:266
  697.0 400.7 %reduce-scatter.24.cloned.1.call-start = ((), (), s32[]{:S(2)}) async-start(), calls=%async_computation.21 | async-start | bytes 4325376 | tf_op jit(solution)/shard_map/reduce_scatter | solution.py:265
  713.9 523.7 %reduce-scatter.20.cloned.1.call-start = ((), (), s32[]{:S(2)}) async-start(), calls=%async_computation.19 | async-start | bytes 4325376 | tf_op jit(solution)/shard_map/reduce_scatter | solution.py:263
  742.2 635.1 %reduce-scatter.22.cloned.1.call-start = ((), (), s32[]{:S(2)}) async-start(), calls=%async_computation.20 | async-start | bytes 4325376 | tf_op jit(solution)/shard_map/reduce_scatter | solution.py:264
  746.1 70.0 %copy-start.1 = (f32[16,64,512]{2,1,0:T(8,128)S(1)}, f32[16,64,512]{2,1,0:T(8,128)}, u32[]{:S(2)}) copy-start(f32[16,64,512]{2,1,0:T(8,128)} %copy-done) | copy-start | bytes 6291460
  (25 other events, 206.5 us)
Sparse Core Ops, SparseCore 0:
  10.9 59.1 all-gather.8
  72.9 55.2 all-gather.10
  131.1 55.2 all-gather.12
  189.0 55.2 all-gather.14
  246.0 24.1 all-gather.20
  272.2 116.6 all-gather.16
  390.8 23.7 all-gather.18
  416.5 25.2 all-gather.22
  463.3 144.4 reduce-scatter.17
  609.9 77.4 reduce-scatter.15
  691.1 38.9 reduce-scatter.31
  733.6 38.4 reduce-scatter.29
  775.8 38.4 reduce-scatter.27
  817.1 141.0 reduce-scatter.25
  961.0 136.6 reduce-scatter.23
  1100.5 137.0 reduce-scatter.19
  1240.4 136.8 reduce-scatter.21
